TPU v7x, 32 devices: a whole 2x2x4 slice. The times are simulated.
32 devices in a mesh: row: 8 (over y, x, core), col: 4 (over z).
Axes of the slice: x: 2, y: 2, z: 4, core: 2. Of those that a mesh axis runs over, the one named last changes fastest.
Arguments:
- traces: bfloat16 [4096, 782], P(('row', 'col')), may hold values from -60 to 60
- taps: float32 [16], replicated, may hold values from -1.5 to 1.5
Outputs:
- correlations: float32 [32, 4096, 4096], P(None, 'row', 'col')
All inputs are finite; a program needn't handle non-finite values.
Results may differ from a plain program's by a relative error of at most 0.0036.
Values may be sent and summed in bfloat16 or wider, within the bound.
A program may use at most 256 MiB of HBM per device.

v0:
```python
import math
import jax
import jax.numpy as jnp
from jax import lax
from jax.sharding import PartitionSpec as P

LAGS = 32


def from_root(array, axis, root):
    mine = lax.axis_index(axis) == root
    return lax.psum(jnp.where(mine, array, jnp.zeros_like(array)), axis)


def whiten(traces, taps, count):
    samples = traces.astype(jnp.float32)
    decimated = jnp.zeros((samples.shape[0], count), jnp.float32)
    for k in range(taps.shape[0]):
        decimated = decimated + taps[k] * samples[:, k : k + 2 * count - 1 : 2]
    centred = decimated - jnp.mean(decimated, axis=1, keepdims=True)
    spread = jnp.sqrt(jnp.mean(centred * centred, axis=1, keepdims=True) + 1e-06)
    return (centred / spread).astype(jnp.bfloat16)


def on_device(traces, taps):
    count = (traces.shape[1] - taps.shape[0] + 2) // 2
    factor = lax.axis_size("row") // lax.axis_size("col")
    column = lax.axis_index("col")
    source = lax.all_gather(traces, "col", axis=0, tiled=True)
    first_block = whiten(source, taps, count)
    pieces = [from_root(source, "row", factor * column + k) for k in range(factor)]
    second_block = jnp.concatenate(pieces, axis=0)
    second_block = whiten(second_block, taps, count)
    lag_count = LAGS
    width = count - lag_count + 1
    scale_factor = 1.0 / math.sqrt(width)
    left = first_block[:, :width]
    groups = []
    for group in range(lag_count // 8):
        shifted = jnp.stack(
            [second_block[:, group * 8 + lag : group * 8 + lag + width] for lag in range(8)], axis=0
        )
        product = jnp.einsum("in,ljn->lij", left, shifted, preferred_element_type=jnp.float32)
        groups.append(product * scale_factor)
    return jnp.concatenate(groups, axis=0)


def solution(mesh):
    placed = (P(("row", "col"), None), P())
    return jax.shard_map(
        on_device, mesh=mesh, in_specs=placed, out_specs=P(None, "row", "col"), check_vma=False
    )
```

profile of v0, /device:TPU:0, one launch (start us, length us, event | category | flops | bytes accessed | tf_op | source)
XLA Modules:
  0.0 332.4 jit_solution(4783237983157764529)
XLA Ops:
  6.5 0.0 all-reduce.3.cloned.1.call-start
  6.5 20.8 %all_gather.3 = bf16[512,782]{0,1:T(8,128)(2,1)S(1)} all-gather(bf16[128,782]{0,1:T(8,128)(2,1)} %param.2), channel_id=1, replica_groups=mesh['row'=8,'col'=4] {'col'}, dimensions={0}, use_global_device_ids=true | all-gather | bytes 1000960 | tf_op jit(solution)/shard_map/all_gather | solution.py:29
  27.3 1.3 broadcast_select_fusion.1
  28.6 0.0 all-reduce.3.cloned.1.call-update
  28.6 0.9 slice.301
  29.5 0.9 slice.302
  30.4 0.9 slice.303
  31.3 2.9 slice.304
  34.2 2.8 slice.305
  37.1 2.8 slice.306
  39.9 2.8 slice.307
  42.7 2.8 slice.308
  45.5 2.8 slice.309
  48.4 2.9 slice.310
  51.2 2.9 slice.311
  54.1 2.9 slice.312
  57.0 2.9 slice.313
  59.8 2.8 slice.314
  62.6 2.8 slice.299
  65.4 2.8 slice.300
  68.2 0.0 copy-done.4
  68.2 0.7 fusion.39
  68.9 15.6 %fusion.37 = (f32[512]{0:T(512)S(1)}, f32[512,384]{0,1:T(8,128)S(1)}) fusion(f32[512,384]{0,1:T(8,128)} %slice.314, f32[]{:T(128)} %bitcast.15, f32[512,384]{0,1:T(8,128)} %slice.313, f32[]{:T(128)} %bitcast.14, f32[512,384]{0,1:T(8,128)} %slice.312, f32[]{:T(128)} %bitcast.13, f32[512,384]{0,1:T(8,128)} %slice.311, f32[]{:T(128)} %bitcast.12, ...), kind=kLoop, calls=%fused_computation.88 | loop fusion | flops 6290944 | bytes 13371456 | tf_op jit(solution)/shard_map/reduce_sum | solution.py:20
  84.5 0.1 multiply_reduce_fusion.1
  84.6 0.9 fusion.24
  85.5 1.4 all-reduce.3.cloned.1.call-done
  86.9 1.8 maximum_convert_fusion
  88.7 4.3 %slice.290 = f32[1024,384]{0,1:T(8,128)} slice(f32[1024,782]{0,1:T(8,128)S(1)} %maximum_convert_fusion), slice={[0:1024:1], [15:782:2]} | slice | bytes 3145728 | tf_op jit(solution)/shard_map/slice | solution.py:19
  93.0 4.3 %slice.288 = f32[1024,384]{0,1:T(8,128)} slice(f32[1024,782]{0,1:T(8,128)S(1)} %maximum_convert_fusion), slice={[0:1024:1], [14:781:2]} | slice | bytes 3145728 | tf_op jit(solution)/shard_map/slice | solution.py:19
  97.3 4.3 %slice.286 = f32[1024,384]{0,1:T(8,128)} slice(f32[1024,782]{0,1:T(8,128)S(1)} %maximum_convert_fusion), slice={[0:1024:1], [13:780:2]} | slice | bytes 3145728 | tf_op jit(solution)/shard_map/slice | solution.py:19
  101.6 4.3 %slice.284 = f32[1024,384]{0,1:T(8,128)} slice(f32[1024,782]{0,1:T(8,128)S(1)} %maximum_convert_fusion), slice={[0:1024:1], [12:779:2]} | slice | bytes 3145728 | tf_op jit(solution)/shard_map/slice | solution.py:19
  105.9 4.4 %slice.282 = f32[1024,384]{0,1:T(8,128)} slice(f32[1024,782]{0,1:T(8,128)S(1)} %maximum_convert_fusion), slice={[0:1024:1], [11:778:2]} | slice | bytes 3145728 | tf_op jit(solution)/shard_map/slice | solution.py:19
  110.2 4.3 %slice.280 = f32[1024,384]{0,1:T(8,128)} slice(f32[1024,782]{0,1:T(8,128)S(1)} %maximum_convert_fusion), slice={[0:1024:1], [10:777:2]} | slice | bytes 3145728 | tf_op jit(solution)/shard_map/slice | solution.py:19
  114.5 4.3 %slice.278 = f32[1024,384]{0,1:T(8,128)} slice(f32[1024,782]{0,1:T(8,128)S(1)} %maximum_convert_fusion), slice={[0:1024:1], [9:776:2]} | slice | bytes 3145728 | tf_op jit(solution)/shard_map/slice | solution.py:19
  118.8 4.2 %slice.276 = f32[1024,384]{0,1:T(8,128)} slice(f32[1024,782]{0,1:T(8,128)S(1)} %maximum_convert_fusion), slice={[0:1024:1], [8:775:2]} | slice | bytes 3145728 | tf_op jit(solution)/shard_map/slice | solution.py:19
  123.0 4.3 %slice.274 = f32[1024,384]{0,1:T(8,128)} slice(f32[1024,782]{0,1:T(8,128)S(1)} %maximum_convert_fusion), slice={[0:1024:1], [7:774:2]} | slice | bytes 3145728 | tf_op jit(solution)/shard_map/slice | solution.py:19
  127.3 4.3 %slice.272 = f32[1024,384]{0,1:T(8,128)} slice(f32[1024,782]{0,1:T(8,128)S(1)} %maximum_convert_fusion), slice={[0:1024:1], [6:773:2]} | slice | bytes 3145728 | tf_op jit(solution)/shard_map/slice | solution.py:19
  131.6 4.3 %slice.270 = f32[1024,384]{0,1:T(8,128)} slice(f32[1024,782]{0,1:T(8,128)S(1)} %maximum_convert_fusion), slice={[0:1024:1], [5:772:2]} | slice | bytes 3145728 | tf_op jit(solution)/shard_map/slice | solution.py:19
  135.9 4.3 %slice.268 = f32[1024,384]{0,1:T(8,128)} slice(f32[1024,782]{0,1:T(8,128)S(1)} %maximum_convert_fusion), slice={[0:1024:1], [4:771:2]} | slice | bytes 3145728 | tf_op jit(solution)/shard_map/slice | solution.py:19
  140.2 4.3 %slice.266 = f32[1024,384]{0,1:T(8,128)} slice(f32[1024,782]{0,1:T(8,128)S(1)} %maximum_convert_fusion), slice={[0:1024:1], [3:770:2]} | slice | bytes 3145728 | tf_op jit(solution)/shard_map/slice | solution.py:19
  144.6 4.3 %slice.264 = f32[1024,384]{0,1:T(8,128)} slice(f32[1024,782]{0,1:T(8,128)S(1)} %maximum_convert_fusion), slice={[0:1024:1], [2:769:2]} | slice | bytes 3145728 | tf_op jit(solution)/shard_map/slice | solution.py:19
  148.9 4.2 %slice.262 = f32[1024,384]{0,1:T(8,128)} slice(f32[1024,782]{0,1:T(8,128)S(1)} %maximum_convert_fusion), slice={[0:1024:1], [1:768:2]} | slice | bytes 3145728 | tf_op jit(solution)/shard_map/slice | solution.py:19
  153.1 4.2 %slice.260 = f32[1024,384]{0,1:T(8,128)} slice(f32[1024,782]{0,1:T(8,128)S(1)} %maximum_convert_fusion), slice={[0:1024:1], [0:767:2]} | slice | bytes 3145728 | tf_op jit(solution)/shard_map/slice | solution.py:19
  157.3 21.6 %fusion.38 = (f32[1024]{0:T(1024)S(1)}, f32[1024,384]{0,1:T(8,128)S(1)}) fusion(f32[1024,384]{0,1:T(8,128)} %slice.290, f32[]{:T(128)} %bitcast.15, f32[1024,384]{0,1:T(8,128)} %slice.288, f32[]{:T(128)} %bitcast.14, f32[1024,384]{0,1:T(8,128)} %slice.286, f32[]{:T(128)} %bitcast.13, f32[1024,384]{0,1:T(8,128)} %slice.284, f32[]{:T(128)} %bitcast.12, ...), kind=kLoop, calls=%fused_computation.89 | loop fusion | flops 12581888 | bytes 26742848 | tf_op jit(solution)/shard_map/reduce_sum | solution.py:20
  178.9 0.2 multiply_reduce_fusion
  179.2 0.2 divide_convert_fusion
  179.4 0.3 fusion.32
  179.7 0.4 fusion.31
  180.1 0.4 fusion.30
  180.5 0.4 fusion.29
  180.9 0.4 fusion.28
  181.3 0.4 fusion.27
  181.7 0.0 copy-start.3
  181.7 0.4 fusion.26
  182.1 0.4 fusion.25
  182.6 2.6 copy-done
  185.1 2.5 copy-done.2
  187.7 5.1 %multiply_bitcast_fusion.3 = f32[8,512,1024]{1,2,0:T(8,128)S(1)} fusion(bf16[8,1024,353]{1,2,0:T(8,128)(2,1)S(1)} %get-tuple-element.15, bf16[512,353]{0,1:T(8,128)(2,1)S(1)} %copy-done.3), kind=kOutput, calls=%fused_computation.4 | convolution fusion | flops 2965372928 | bytes 22922240 | tf_op jit(solution)/shard_map/in,ljn->lij/dot_general | solution.py:43
  192.8 0.0 slice-start
  192.8 9.0 %multiply_bitcast_fusion = f32[8,512,1024]{1,2,0:T(8,128)} fusion(bf16[8,1024,353]{1,2,0:T(8,128)(2,1)S(1)} %get-tuple-element.16, bf16[512,353]{0,1:T(8,128)(2,1)S(1)} %copy-done.3), kind=kOutput, calls=%fused_computation.1 | convolution fusion | flops 2965372928 | bytes 22922240 | tf_op jit(solution)/shard_map/in,ljn->lij/dot_general | solution.py:43
  201.9 8.5 %multiply_bitcast_fusion.1 = f32[8,512,1024]{1,2,0:T(8,128)} fusion(bf16[8,1024,353]{1,2,0:T(8,128)(2,1)S(1)} %copy-done.1, bf16[512,353]{0,1:T(8,128)(2,1)S(1)} %copy-done.3), kind=kOutput, calls=%fused_computation.2 | convolution fusion | flops 2965372928 | bytes 22922240 | tf_op jit(solution)/shard_map/in,ljn->lij/dot_general | solution.py:43
  210.4 8.5 %multiply_bitcast_fusion.2 = f32[8,512,1024]{1,2,0:T(8,128)} fusion(bf16[8,1024,353]{1,2,0:T(8,128)(2,1)S(1)} %bitcast.166, bf16[512,353]{0,1:T(8,128)(2,1)S(1)} %copy-done.3), kind=kOutput, calls=%fused_computation.3 | convolution fusion | flops 2965372928 | bytes 22922240 | tf_op jit(solution)/shard_map/in,ljn->lij/dot_general | solution.py:43
  218.8 40.9 %pad_maximum_fusion = f32[32,512,1024]{1,2,0:T(8,128)} fusion(f32[8,512,1024]{1,2,0:T(8,128)} %multiply_bitcast_fusion, f32[8,512,1024]{1,2,0:T(8,128)} %multiply_bitcast_fusion.1, f32[8,512,1024]{1,2,0:T(8,128)} %multiply_bitcast_fusion.2, f32[8,512,1024]{1,2,0:T(8,128)S(1)} %multiply_bitcast_fusion.3), kind=kLoop, calls=%fused_computation | loop fusion | flops 50331648 | bytes 134217728 | tf_op jit(solution)/shard_map/concatenate | solution.py:45
  259.7 65.8 %copy.3 = f32[32,512,1024]{2,1,0:T(8,128)} copy(f32[32,512,1024]{1,2,0:T(8,128)} %pad_maximum_fusion) | data formatting | bytes 134217728 | tf_op jit(solution)/shard_map/concatenate | solution.py:45
  (14 shorter events, 0.0 us)
Async XLA Ops:
  6.5 80.3 %all-reduce.3.cloned.1.call-start = ((), (), s32[]{:S(2)}) async-start(), calls=%async_computation | async-start | bytes 3211264 | tf_op jit(solution)/shard_map/psum | solution.py:12
  48.4 19.8 %copy-start.4 = (f32[16]{0:T(128)S(1)}, f32[16]{0:T(128)}, u32[]{:S(2)}) copy-start(f32[16]{0:T(128)} %param.3) | copy-start | bytes 196
  181.7 5.9 %copy-start.3 = (bf16[512,353]{0,1:T(8,128)(2,1)S(1)}, bf16[512,353]{0,1:T(8,128)(2,1)}, u32[]{:S(2)}) copy-start(bf16[512,353]{0,1:T(8,128)(2,1)} %fusion.24) | copy-start | bytes 1084420
  182.5 2.6 copy-start
  185.1 2.5 copy-start.2
  192.8 9.1 %copy-start.1 = (bf16[8,1024,353]{1,2,0:T(8,128)(2,1)S(1)}, bf16[8,1024,353]{1,2,0:T(8,128)(2,1)}, u32[]{:S(2)}) copy-start(bf16[8,1024,353]{1,2,0:T(8,128)(2,1)} %copy-done) | copy-start | bytes 17350660
  192.8 17.5 %slice-start = ((s8[5898240]{0:T(1024)(128)(4,1)}), s8[1703936]{0:T(1024)(128)(4,1)S(1)}, s32[]{:S(2)}) async-start(s8[5898240]{0:T(1024)(128)(4,1)} %bitcast.165), calls=%async_computation.1 | async-start | bytes 3407872
  201.9 8.5 %slice-start.1 = ((s8[5898240]{0:T(1024)(128)(4,1)}), s8[4194304]{0:T(1024)(128)(4,1)S(1)}, s32[]{:S(2)}) async-start(s8[5898240]{0:T(1024)(128)(4,1)} %bitcast.165), calls=%async_computation.2 | async-start | bytes 8388608
Sparse Core Ops, SparseCore 0:
  28.8 58.0 all-reduce.2
where the time goes:
time: 334 us; the launch traced here: 332 us
  local copies, waits for them, and re-layouts  183 us (55%)
  other arithmetic  82.7 us (25%)
  matrix products  31.1 us (9%)
  blocking collectives  20.8 us (6%)
  between operations  13.6 us (4%)
    slice x33, local copies, waits for them, and re-layouts, whiten(): decimated = decimated + taps[k] * samples[:, k:k + 2 * count - 1:2]  109 us
    concatenate x1, local copies, waits for them, and re-layouts, on_device(): return jnp.concatenate(groups, axis=0)  65.8 us
    concatenate x1, other arithmetic, on_device(): return jnp.concatenate(groups, axis=0)  40.9 us
    reduce_sum x2, other arithmetic, whiten(): centred = decimated - jnp.mean(decimated, axis=1, keepdims=True)  37.2 us
    dot_general x4, matrix products, on_device(): jnp.einsum('in,ljn->lij', left, shifted, preferred_element_type=jnp.float32)  31.1 us
    all_gather x1, blocking collectives, on_device(): source = lax.all_gather(traces, 'col', axis=0, tiled=True)  20.8 us
    unnamed x21, local copies, waits for them, and re-layouts  7.78 us
  transfers between devices with their start and end apart: 1, of which 1 were waited for; matrix products, arithmetic and copies ran while one was open for 17% of the time, Pallas kernels for 0%

commit v1 on v0

--- a/solution.py
+++ b/solution.py
@@ -5,6 +5,27 @@
 from jax.sharding import PartitionSpec as P
 
 LAGS = 32
+
+
+def gather_around(x, axis, dim):
+    length, index, extent = (lax.axis_size(axis), lax.axis_index(axis), x.shape[dim])
+    right = [(i, (i + 1) % length) for i in range(length)]
+    behind = [(i, (i - 1) % length) for i in range(length)]
+    out = jnp.zeros((*x.shape[:dim], length * extent, *x.shape[dim + 1 :]), x.dtype)
+    out = lax.dynamic_update_slice_in_dim(out, x, index * extent, axis=dim)
+    from_left = from_right = x
+    middle = length // 2
+    for hop in range(1, middle + 1):
+        from_left = lax.ppermute(from_left, axis, right)
+        out = lax.dynamic_update_slice_in_dim(
+            out, from_left, (index - hop) % length * extent, axis=dim
+        )
+        if hop < length - middle:
+            from_right = lax.ppermute(from_right, axis, behind)
+            out = lax.dynamic_update_slice_in_dim(
+                out, from_right, (index + hop) % length * extent, axis=dim
+            )
+    return out
 
 
 def from_root(array, axis, root):
@@ -26,7 +47,7 @@
     count = (traces.shape[1] - taps.shape[0] + 2) // 2
     factor = lax.axis_size("row") // lax.axis_size("col")
     column = lax.axis_index("col")
-    source = lax.all_gather(traces, "col", axis=0, tiled=True)
+    source = gather_around(traces, "col", 0)
     first_block = whiten(source, taps, count)
     pieces = [from_root(source, "row", factor * column + k) for k in range(factor)]
     second_block = jnp.concatenate(pieces, axis=0)

time: 334 us -> 374 us (1.12)
  waiting for transfers between devices: 1.4 us -> 53.7 us
  blocking collectives: 20.8 us -> 0 us
  starting transfers between devices: 0.01 us -> 6.68 us
    psum x1, waiting for transfers between devices: 1.39 us -> 41.2 us  [from_root(): return lax.psum(jnp.where(mine, array, jnp.zeros_like(array)), axis)]
    all_gather x1 -> x0, blocking collectives: 20.8 us -> none  [on_device(): source = lax.all_gather(traces, 'col', axis=0, tiled=True)]
    ppermute x0 -> x3, waiting for transfers between devices: none -> 12.6 us  [the longest x2 12.6 us: gather_around(): from_left = lax.ppermute(from_left, axis, right)]
    ppermute x0 -> x3, starting transfers between devices: none -> 6.67 us  [the longest x1 5.05 us: gather_around(): from_right = lax.ppermute(from_right, axis, behind)]
    unnamed x21 -> x19, local copies, waits for them, and re-layouts: 7.78 us -> 7.78 us
  transfers between devices with their start and end apart: 1 -> 4, of which waited for: 1 -> 3; matrix products, arithmetic and copies ran while one was open for 17% -> 5% of each run, Pallas kernels for 0% -> 0%
where the time goes in v1:
time: 374 us; the launch traced here: 373 us
  local copies, waits for them, and re-layouts  185 us (49%)
  other arithmetic  82.6 us (22%)
  waiting for transfers between devices  53.7 us (14%)
  matrix products  31.2 us (8%)
  between operations  13.6 us (4%)
  starting transfers between devices  6.68 us (2%)
    slice x33, local copies, waits for them, and re-layouts, whiten(): decimated = decimated + taps[k] * samples[:, k:k + 2 * count - 1:2]  110 us
    concatenate x1, local copies, waits for them, and re-layouts, on_device(): return jnp.concatenate(groups, axis=0)  65.8 us
    psum x1, waiting for transfers between devices, from_root(): return lax.psum(jnp.where(mine, array, jnp.zeros_like(array)), axis)  41.2 us
    concatenate x1, other arithmetic, on_device(): return jnp.concatenate(groups, axis=0)  40.9 us
    reduce_sum x2, other arithmetic, whiten(): centred = decimated - jnp.mean(decimated, axis=1, keepdims=True)  37.2 us
    dot_general x4, matrix products, on_device(): jnp.einsum('in,ljn->lij', left, shifted, preferred_element_type=jnp.float32)  31.2 us
    ppermute x2, waiting for transfers between devices, gather_around(): from_left = lax.ppermute(from_left, axis, right)  12.6 us
    unnamed x19, local copies, waits for them, and re-layouts  7.78 us
  transfers between devices with their start and end apart: 4, of which 3 were waited for; matrix products, arithmetic and copies ran while one was open for 5% of the time, Pallas kernels for 0%

profile of v1, /device:TPU:0, one launch (start us, length us, event | category | flops | bytes accessed | tf_op | source)
XLA Modules:
  0.0 373.0 jit_solution(14233011276068738594)
XLA Ops:
  6.5 5.0 %collective-permute-start.1 = (bf16[128,782]{0,1:T(8,128)(2,1)}, bf16[128,782]{0,1:T(8,128)(2,1)S(1)}, u32[]{:S(2)}, u32[]{:S(2)}) collective-permute-start(bf16[128,782]{0,1:T(8,128)(2,1)} %param.2), channel_id=1, source_target_pairs={{0,3},{1,0},{2,1},{3,2},{4,7},{5,4},{6,5},{7,6},{8,11},{9,8},{10,9... | collective-permute-start | bytes 600584 | tf_op jit(solution)/shard_map/ppermute | solution.py:24
  11.6 0.1 broadcast.54
  11.6 1.0 constant_dynamic-update-slice_fusion.3
  12.6 1.9 fusion.39
  14.6 6.7 %collective-permute-done = bf16[128,782]{0,1:T(8,128)(2,1)S(1)} collective-permute-done((bf16[128,782]{0,1:T(8,128)(2,1)}, bf16[128,782]{0,1:T(8,128)(2,1)S(1)}, u32[]{:S(2)}, u32[]{:S(2)}) %collective-permute-start) | collective-permute-done | bytes 200224 | tf_op jit(solution)/shard_map/ppermute | solution.py:19
  21.3 1.6 collective-permute-start.2
  23.0 5.9 %collective-permute-done.2 = bf16[128,782]{0,1:T(8,128)(2,1)S(1)} collective-permute-done((bf16[128,782]{0,1:T(8,128)(2,1)S(1)}, bf16[128,782]{0,1:T(8,128)(2,1)S(1)}, u32[]{:S(2)}, u32[]{:S(2)}) %collective-permute-start.2) | collective-permute-done | bytes 200224 | tf_op jit(solution)/shard_map/ppermute | solution.py:19
  29.0 0.9 slice.301
  29.9 0.9 slice.302
  30.8 0.9 slice.303
  31.7 2.9 slice.304
  34.5 2.8 slice.305
  37.4 2.8 slice.306
  40.2 2.8 slice.307
  43.0 2.8 slice.308
  45.8 2.9 slice.309
  48.7 2.9 slice.310
  51.5 2.8 slice.311
  54.4 2.9 slice.312
  57.2 2.8 slice.313
  60.1 2.8 slice.314
  62.9 2.8 slice.299
  65.7 2.7 slice.300
  68.4 1.3 broadcast_select_fusion.1
  69.7 15.6 %fusion.37 = (f32[512]{0:T(512)S(1)}, f32[512,384]{0,1:T(8,128)S(1)}) fusion(f32[512,384]{0,1:T(8,128)} %slice.314, f32[]{:T(128)} %bitcast.15, f32[512,384]{0,1:T(8,128)} %slice.313, f32[]{:T(128)} %bitcast.14, f32[512,384]{0,1:T(8,128)} %slice.312, f32[]{:T(128)} %bitcast.13, f32[512,384]{0,1:T(8,128)} %slice.311, f32[]{:T(128)} %bitcast.12, ...), kind=kLoop, calls=%fused_computation.92 | loop fusion | flops 6290944 | bytes 13371456 | tf_op jit(solution)/shard_map/reduce_sum | solution.py:41
  85.2 0.1 multiply_reduce_fusion.1
  85.4 0.8 fusion.24
  86.2 41.2 %all-reduce.3.cloned.1.call-done = (bf16[512,782]{0,1:T(8,128)(2,1)}, bf16[512,782]{0,1:T(8,128)(2,1)}) async-done(((bf16[512,782]{0,1:T(8,128)(2,1)}, bf16[512,782]{0,1:T(8,128)(2,1)}), (bf16[512,782]{0,1:T(8,128)(2,1)}, bf16[512,782]{0,1:T(8,128)(2,1)})) %all-reduce.3.cloned.1.call-update) | async-done | bytes 1601552 | tf_op jit(solution)/shard_map/psum | solution.py:33
  127.4 1.8 maximum_convert_fusion
  129.2 4.3 %slice.290 = f32[1024,384]{0,1:T(8,128)} slice(f32[1024,782]{0,1:T(8,128)S(1)} %maximum_convert_fusion), slice={[0:1024:1], [15:782:2]} | slice | bytes 3145728 | tf_op jit(solution)/shard_map/slice | solution.py:40
  133.5 4.3 %slice.288 = f32[1024,384]{0,1:T(8,128)} slice(f32[1024,782]{0,1:T(8,128)S(1)} %maximum_convert_fusion), slice={[0:1024:1], [14:781:2]} | slice | bytes 3145728 | tf_op jit(solution)/shard_map/slice | solution.py:40
  137.8 4.3 %slice.286 = f32[1024,384]{0,1:T(8,128)} slice(f32[1024,782]{0,1:T(8,128)S(1)} %maximum_convert_fusion), slice={[0:1024:1], [13:780:2]} | slice | bytes 3145728 | tf_op jit(solution)/shard_map/slice | solution.py:40
  142.1 4.3 %slice.284 = f32[1024,384]{0,1:T(8,128)} slice(f32[1024,782]{0,1:T(8,128)S(1)} %maximum_convert_fusion), slice={[0:1024:1], [12:779:2]} | slice | bytes 3145728 | tf_op jit(solution)/shard_map/slice | solution.py:40
  146.4 4.4 %slice.282 = f32[1024,384]{0,1:T(8,128)} slice(f32[1024,782]{0,1:T(8,128)S(1)} %maximum_convert_fusion), slice={[0:1024:1], [11:778:2]} | slice | bytes 3145728 | tf_op jit(solution)/shard_map/slice | solution.py:40
  150.8 4.3 %slice.280 = f32[1024,384]{0,1:T(8,128)} slice(f32[1024,782]{0,1:T(8,128)S(1)} %maximum_convert_fusion), slice={[0:1024:1], [10:777:2]} | slice | bytes 3145728 | tf_op jit(solution)/shard_map/slice | solution.py:40
  155.1 4.2 %slice.278 = f32[1024,384]{0,1:T(8,128)} slice(f32[1024,782]{0,1:T(8,128)S(1)} %maximum_convert_fusion), slice={[0:1024:1], [9:776:2]} | slice | bytes 3145728 | tf_op jit(solution)/shard_map/slice | solution.py:40
  159.4 4.2 %slice.276 = f32[1024,384]{0,1:T(8,128)} slice(f32[1024,782]{0,1:T(8,128)S(1)} %maximum_convert_fusion), slice={[0:1024:1], [8:775:2]} | slice | bytes 3145728 | tf_op jit(solution)/shard_map/slice | solution.py:40
  163.6 4.3 %slice.274 = f32[1024,384]{0,1:T(8,128)} slice(f32[1024,782]{0,1:T(8,128)S(1)} %maximum_convert_fusion), slice={[0:1024:1], [7:774:2]} | slice | bytes 3145728 | tf_op jit(solution)/shard_map/slice | solution.py:40
  167.9 4.3 %slice.272 = f32[1024,384]{0,1:T(8,128)} slice(f32[1024,782]{0,1:T(8,128)S(1)} %maximum_convert_fusion), slice={[0:1024:1], [6:773:2]} | slice | bytes 3145728 | tf_op jit(solution)/shard_map/slice | solution.py:40
  172.2 4.3 %slice.270 = f32[1024,384]{0,1:T(8,128)} slice(f32[1024,782]{0,1:T(8,128)S(1)} %maximum_convert_fusion), slice={[0:1024:1], [5:772:2]} | slice | bytes 3145728 | tf_op jit(solution)/shard_map/slice | solution.py:40
  176.5 4.3 %slice.268 = f32[1024,384]{0,1:T(8,128)} slice(f32[1024,782]{0,1:T(8,128)S(1)} %maximum_convert_fusion), slice={[0:1024:1], [4:771:2]} | slice | bytes 3145728 | tf_op jit(solution)/shard_map/slice | solution.py:40
  180.8 4.3 %slice.266 = f32[1024,384]{0,1:T(8,128)} slice(f32[1024,782]{0,1:T(8,128)S(1)} %maximum_convert_fusion), slice={[0:1024:1], [3:770:2]} | slice | bytes 3145728 | tf_op jit(solution)/shard_map/slice | solution.py:40
  185.2 4.3 %slice.264 = f32[1024,384]{0,1:T(8,128)} slice(f32[1024,782]{0,1:T(8,128)S(1)} %maximum_convert_fusion), slice={[0:1024:1], [2:769:2]} | slice | bytes 3145728 | tf_op jit(solution)/shard_map/slice | solution.py:40
  189.5 4.2 %slice.262 = f32[1024,384]{0,1:T(8,128)} slice(f32[1024,782]{0,1:T(8,128)S(1)} %maximum_convert_fusion), slice={[0:1024:1], [1:768:2]} | slice | bytes 3145728 | tf_op jit(solution)/shard_map/slice | solution.py:40
  193.7 4.2 %slice.260 = f32[1024,384]{0,1:T(8,128)} slice(f32[1024,782]{0,1:T(8,128)S(1)} %maximum_convert_fusion), slice={[0:1024:1], [0:767:2]} | slice | bytes 3145728 | tf_op jit(solution)/shard_map/slice | solution.py:40
  197.9 21.6 %fusion.38 = (f32[1024]{0:T(1024)S(1)}, f32[1024,384]{0,1:T(8,128)S(1)}) fusion(f32[1024,384]{0,1:T(8,128)} %slice.290, f32[]{:T(128)} %bitcast.15, f32[1024,384]{0,1:T(8,128)} %slice.288, f32[]{:T(128)} %bitcast.14, f32[1024,384]{0,1:T(8,128)} %slice.286, f32[]{:T(128)} %bitcast.13, f32[1024,384]{0,1:T(8,128)} %slice.284, f32[]{:T(128)} %bitcast.12, ...), kind=kLoop, calls=%fused_computation.93 | loop fusion | flops 12581888 | bytes 26742848 | tf_op jit(solution)/shard_map/reduce_sum | solution.py:41
  219.6 0.2 multiply_reduce_fusion
  219.8 0.2 divide_convert_fusion
  220.0 0.3 fusion.32
  220.4 0.4 fusion.31
  220.8 0.4 fusion.30
  221.2 0.4 fusion.29
  221.6 0.4 fusion.28
  222.0 0.4 fusion.27
  222.4 0.4 fusion.26
  222.8 0.4 fusion.25
  223.2 2.6 copy-done
  225.7 2.5 copy-done.2
  228.3 5.1 %multiply_bitcast_fusion.3 = f32[8,512,1024]{1,2,0:T(8,128)S(1)} fusion(bf16[8,1024,353]{1,2,0:T(8,128)(2,1)S(1)} %get-tuple-element.15, bf16[512,353]{0,1:T(8,128)(2,1)S(1)} %copy-done.3), kind=kOutput, calls=%fused_computation.4 | convolution fusion | flops 2965372928 | bytes 22922240 | tf_op jit(solution)/shard_map/in,ljn->lij/dot_general | solution.py:64
  233.4 9.0 %multiply_bitcast_fusion = f32[8,512,1024]{1,2,0:T(8,128)} fusion(bf16[8,1024,353]{1,2,0:T(8,128)(2,1)S(1)} %get-tuple-element.16, bf16[512,353]{0,1:T(8,128)(2,1)S(1)} %copy-done.3), kind=kOutput, calls=%fused_computation.1 | convolution fusion | flops 2965372928 | bytes 22922240 | tf_op jit(solution)/shard_map/in,ljn->lij/dot_general | solution.py:64
  242.5 8.5 %multiply_bitcast_fusion.1 = f32[8,512,1024]{1,2,0:T(8,128)} fusion(bf16[8,1024,353]{1,2,0:T(8,128)(2,1)S(1)} %copy-done.1, bf16[512,353]{0,1:T(8,128)(2,1)S(1)} %copy-done.3), kind=kOutput, calls=%fused_computation.2 | convolution fusion | flops 2965372928 | bytes 22922240 | tf_op jit(solution)/shard_map/in,ljn->lij/dot_general | solution.py:64
  251.0 8.5 %multiply_bitcast_fusion.2 = f32[8,512,1024]{1,2,0:T(8,128)} fusion(bf16[8,1024,353]{1,2,0:T(8,128)(2,1)S(1)} %bitcast.166, bf16[512,353]{0,1:T(8,128)(2,1)S(1)} %copy-done.3), kind=kOutput, calls=%fused_computation.3 | convolution fusion | flops 2965372928 | bytes 22922240 | tf_op jit(solution)/shard_map/in,ljn->lij/dot_general | solution.py:64
  259.5 40.9 %pad_maximum_fusion = f32[32,512,1024]{1,2,0:T(8,128)} fusion(f32[8,512,1024]{1,2,0:T(8,128)} %multiply_bitcast_fusion, f32[8,512,1024]{1,2,0:T(8,128)} %multiply_bitcast_fusion.1, f32[8,512,1024]{1,2,0:T(8,128)} %multiply_bitcast_fusion.2, f32[8,512,1024]{1,2,0:T(8,128)S(1)} %multiply_bitcast_fusion.3), kind=kLoop, calls=%fused_computation | loop fusion | flops 50331648 | bytes 134217728 | tf_op jit(solution)/shard_map/concatenate | solution.py:66
  300.4 65.8 %copy.3 = f32[32,512,1024]{2,1,0:T(8,128)} copy(f32[32,512,1024]{1,2,0:T(8,128)} %pad_maximum_fusion) | data formatting | bytes 134217728 | tf_op jit(solution)/shard_map/concatenate | solution.py:66
  (22 shorter events, 0.2 us)
Async XLA Ops:
  6.5 120.9 %all-reduce.3.cloned.1.call-start = ((), (), s32[]{:S(2)}) async-start(), calls=%async_computation | async-start | bytes 3211264 | tf_op jit(solution)/shard_map/psum | solution.py:33
  6.5 16.4 %collective-permute-start.1 = (bf16[128,782]{0,1:T(8,128)(2,1)}, bf16[128,782]{0,1:T(8,128)(2,1)S(1)}, u32[]{:S(2)}, u32[]{:S(2)}) collective-permute-start(bf16[128,782]{0,1:T(8,128)(2,1)} %param.2), channel_id=1, source_target_pairs={{0,3},{1,0},{2,1},{3,2},{4,7},{5,4},{6,5},{7,6},{8,11},{9,8},{10,9... | collective-permute-start | bytes 600584 | tf_op jit(solution)/shard_map/ppermute | solution.py:24
  11.6 9.7 %collective-permute-start = (bf16[128,782]{0,1:T(8,128)(2,1)}, bf16[128,782]{0,1:T(8,128)(2,1)S(1)}, u32[]{:S(2)}, u32[]{:S(2)}) collective-permute-start(bf16[128,782]{0,1:T(8,128)(2,1)} %param.2), channel_id=1, source_target_pairs={{0,1},{1,2},{2,3},{3,0},{4,5},{5,6},{6,7},{7,4},{8,9},{9,10},{10,1... | collective-permute-start | bytes 600584 | tf_op jit(solution)/shard_map/ppermute | solution.py:19
  21.3 7.7 %collective-permute-start.2 = (bf16[128,782]{0,1:T(8,128)(2,1)S(1)}, bf16[128,782]{0,1:T(8,128)(2,1)S(1)}, u32[]{:S(2)}, u32[]{:S(2)}) collective-permute-start(bf16[128,782]{0,1:T(8,128)(2,1)S(1)} %collective-permute-done), channel_id=1, source_target_pairs={{0,1},{1,2},{2,3},{3,0},{4,5},{5,6},{6,7},{7,4},{8,9},{9,10},{10,1... | collective-permute-start | bytes 600584 | tf_op jit(solution)/shard_map/ppermute | solution.py:19
  222.4 5.9 %copy-start.3 = (bf16[512,353]{0,1:T(8,128)(2,1)S(1)}, bf16[512,353]{0,1:T(8,128)(2,1)}, u32[]{:S(2)}) copy-start(bf16[512,353]{0,1:T(8,128)(2,1)} %fusion.24) | copy-start | bytes 1084420
  223.2 2.6 copy-start
  225.7 2.5 copy-start.2
  233.4 9.1 %copy-start.1 = (bf16[8,1024,353]{1,2,0:T(8,128)(2,1)S(1)}, bf16[8,1024,353]{1,2,0:T(8,128)(2,1)}, u32[]{:S(2)}) copy-start(bf16[8,1024,353]{1,2,0:T(8,128)(2,1)} %copy-done) | copy-start | bytes 17350660
  233.4 17.5 %slice-start = ((s8[5898240]{0:T(1024)(128)(4,1)}), s8[1703936]{0:T(1024)(128)(4,1)S(1)}, s32[]{:S(2)}) async-start(s8[5898240]{0:T(1024)(128)(4,1)} %bitcast.165), calls=%async_computation.1 | async-start | bytes 3407872
  242.5 8.5 %slice-start.1 = ((s8[5898240]{0:T(1024)(128)(4,1)}), s8[4194304]{0:T(1024)(128)(4,1)S(1)}, s32[]{:S(2)}) async-start(s8[5898240]{0:T(1024)(128)(4,1)} %bitcast.165), calls=%async_computation.2 | async-start | bytes 8388608
Sparse Core Ops, SparseCore 0:
  69.8 57.5 all-reduce.2
